TPU v7x, 128 devices: a whole 4x4x4 slice. The times are simulated.
128 devices in a mesh: row: 16 (over y_lo, z, core), col: 8 (over x, y_hi).
Axes of the slice: x: 4, y: 4 (y_hi: 2, y_lo: 2; y = y_hi * 2 + y_lo), z: 4, core: 2. Of those that a mesh axis runs over, the one named last changes fastest.
Arguments:
- pair: bfloat16 [768, 768, 128], P('row', 'col'), may hold values from -4 to 4
- token_mask: int32 [768], replicated, may hold values from 0 to 1, as said below
- chain_ids: int32 [768], replicated, may hold values from 0 to 3, as said below
- w_query: bfloat16 [128, 128], replicated, may hold values from -0.5 to 0.5
- w_key: bfloat16 [128, 128], replicated, may hold values from -0.5 to 0.5
- w_value: bfloat16 [128, 128], replicated, may hold values from -0.5 to 0.5
- w_gate: bfloat16 [128, 128], replicated, may hold values from -0.5 to 0.5
- w_bias: bfloat16 [128, 4], replicated, may hold values from -2.5 to 2.5
- w_out: bfloat16 [128, 128], replicated, may hold values from -6 to 6
Outputs:
- update: bfloat16 [768, 768, 128], P('row', 'col')
Inputs may be any that keep to these rules, and one draw needn't show every extreme that they name: `token_mask`: 0 or 1; the first token of every chain is 1. `chain_ids`: never falling along the tokens, every chain nonempty; chain 0 holds at least the first 385 tokens.
All inputs are finite; a program needn't handle non-finite values.
Results may differ from a plain program's by a relative error of at most 0.0095.
Values may be sent and summed in bfloat16 or wider, within the bound.
A program may use at most 192 MiB of HBM per device.

v0:
```python
import math

import jax
import jax.numpy as jnp
from jax import lax
from jax.sharding import PartitionSpec as P


def from_root(block, axis, owner):
    block = jnp.where(lax.axis_index(axis) == owner, block, jnp.zeros_like(block))
    return lax.psum(block, axis)


def normalize(pair):
    values = pair.astype(jnp.float32)
    center = jnp.mean(values, axis=-1, keepdims=True)
    spread = jnp.mean((values - center) ** 2, axis=-1, keepdims=True)
    return ((values - center) * lax.rsqrt(spread + 1e-05)).astype(jnp.bfloat16)


def project(flat, weight, factor):
    return (jnp.dot(flat, weight, preferred_element_type=jnp.float32) * factor).astype(jnp.bfloat16)


def body(pair, token_mask, chain_ids, w_query, w_key, w_value, w_gate, w_bias, w_out):
    rows, cols, width = pair.shape
    heads = w_bias.shape[1]
    inner = w_query.shape[1]
    head_dim = inner // heads
    factor = 1.0 / math.sqrt(head_dim)
    row_index = lax.axis_index("row")
    col_index = lax.axis_index("col")
    normed = normalize(pair)
    flat = normed.reshape(rows * cols, width)
    bias_tile = jnp.dot(flat, w_bias, preferred_element_type=jnp.float32).astype(jnp.bfloat16)
    bias_tile = jnp.transpose(bias_tile.reshape(rows, cols, heads), (2, 0, 1))
    bias_rows = lax.all_gather(bias_tile, "row", axis=1, tiled=True)
    query = project(flat, w_query, factor).reshape(rows, cols, heads, head_dim)
    gate = jax.nn.sigmoid(jnp.dot(flat, w_gate, preferred_element_type=jnp.float32)).reshape(
        rows, cols, inner
    )
    owner = row_index * rows // cols
    local_start = jnp.clip(row_index * rows - col_index * cols, 0, cols - rows)
    picked = lax.dynamic_slice_in_dim(bias_rows, local_start, rows, 2)
    bias_mine = from_root(picked, "col", owner)
    bias_query = jnp.swapaxes(bias_mine, 1, 2)
    my_chain = lax.dynamic_slice_in_dim(chain_ids, col_index * cols, cols)
    key_tile = project(flat, w_key, 1.0).reshape(rows, cols, inner)
    value_tile = project(flat, w_value, 1.0).reshape(rows, cols, inner)
    key_piece = lax.all_gather(key_tile, "row", axis=0, tiled=True)
    running_peak = jnp.full((cols, heads, rows), -1e30, jnp.float32)
    count = key_piece.shape[0]
    key_heads = key_piece.reshape(count, cols, heads, head_dim)
    value_heads = lax.all_gather(value_tile, "row", axis=0, tiled=True).reshape(
        count, cols, heads, head_dim
    )
    scores = jnp.einsum("ijhd,kjhd->jhik", query, key_heads, preferred_element_type=jnp.float32)
    scores = scores + bias_query[None].astype(jnp.float32)
    key_valid = token_mask == 1
    keep = key_valid[None, :] & (chain_ids[None, :] == my_chain[:, None])
    scores = jnp.where(keep[:, None, None, :], scores, jnp.float32(-1e30))
    new_peak = jnp.maximum(running_peak, jnp.max(scores, axis=-1))
    weights = jnp.exp(scores - new_peak[..., None])
    new_total = jnp.sum(weights, axis=-1)
    product = jnp.einsum(
        "jhik,kjhd->jhid",
        weights.astype(jnp.bfloat16),
        value_heads,
        preferred_element_type=jnp.float32,
    )
    attended = product / new_total[..., None]
    attended = jnp.transpose(attended, (2, 0, 1, 3)).reshape(rows, cols, inner)
    gated = (gate * attended).astype(jnp.bfloat16)
    update = jnp.dot(gated.reshape(rows * cols, inner), w_out, preferred_element_type=jnp.float32)
    return update.astype(jnp.bfloat16).reshape(rows, cols, width)


def solution(mesh):
    placed = (P("row", "col", None), P(), P(), P(), P(), P(), P(), P(), P())
    return jax.shard_map(
        body, mesh=mesh, in_specs=placed, out_specs=P("row", "col", None), check_vma=False
    )
```

profile of v0, /device:TPU:6, one launch (start us, length us, event | category | flops | bytes accessed | tf_op | source)
XLA Modules:
  0.0 395.0 jit_solution(7103733010916302202)
XLA Ops:
  7.4 1.9 convert_reduce_fusion
  9.2 2.7 fusion.19
  12.0 1.4 fusion.20
  13.5 0.4 convolution_convert_fusion.3
  13.9 0.1 reshape.87
  14.0 23.1 %all_gather.10 = bf16[4,768,96]{2,0,1:T(4,128)(2,1)S(1)} all-gather(bf16[4,48,96]{2,0,1:T(4,128)(2,1)S(1)} %bitcast.45), channel_id=1, replica_groups=mesh['row'=16,'col'=8] {'row'}, dimensions={1}, use_global_device_ids=true | all-gather | bytes 626688 | tf_op jit(solution)/shard_map/all_gather | solution.py:37
  37.1 0.5 constant_dynamic-slice_fusion
  37.6 0.5 copy.36
  38.2 0.7 select_bitcast_fusion
  38.9 0.0 all-gather.3.cloned.1.call-start
  39.0 1.6 convolution_convert_fusion.2
  40.6 0.0 all-gather.5.cloned.1.call-start
  40.6 1.5 convolution_convert_fusion.1
  42.1 0.4 fusion.13
  42.6 1.6 copy.28
  44.2 2.9 reshape.84
  47.1 5.2 %copy.30 = bf16[48,96,4,32]{0,3,2,1:T(8,128)(2,1)} copy(bf16[48,96,4,32]{1,0,3,2:T(8,128)(2,1)S(1)} %reshape.84) | data formatting | bytes 2359296 | tf_op jit(solution)/shard_map/reshape | solution.py:38
  52.3 0.1 dynamic_slice.6
  52.3 0.1 compare_and_fusion
  52.5 193.0 %all-reduce.2.cloned.1.call-done = bf16[4,48,768]{2,1,0:T(8,128)(2,1)} async-done(((bf16[4,48,768]{2,1,0:T(8,128)(2,1)}), bf16[4,48,768]{2,1,0:T(8,128)(2,1)}) %all-reduce.2.cloned.1.call-update) | async-done | bytes 294928 | tf_op jit(solution)/shard_map/psum | solution.py:11
  245.5 1.0 convert_element_type.41
  246.5 0.0 all-gather.3.cloned.1.call-done
  246.5 24.2 %copy.29 = bf16[768,96,128]{0,2,1:T(8,128)(2,1)} copy(bf16[768,96,128]{2,1,0:T(8,128)(2,1)} %all-gather.3.cloned.1.call-done) | data formatting | bytes 37748736 | tf_op jit(solution)/shard_map/all_gather | solution.py:50
  270.7 26.4 %fusion = (f32[96,4,48]{2,1,0:T(4,128)S(1)}, f32[96,4,48,768]{3,2,1,0:T(8,128)}) fusion(f32[4,48,768]{2,1,0:T(8,128)S(1)} %convert_element_type.41, pred[96,768]{1,0:T(8,128)(4,1)S(1)} %compare_and_fusion, bf16[48,96,4,32]{0,3,2,1:T(8,128)(2,1)} %copy.30, bf16[768,96,4,32]{0,3,2,1:T(8,128)(2,1)} %bitcast.36), kind=kOutput, calls=%fused_computation.2 | convolution fusion | flops 948418560 | bytes 77414400 | tf_op jit(solution)/shard_map/ijhd,kjhd->jhik/dot_general | solution.py:57
  297.1 0.1 broadcast_maximum_fusion
  297.1 19.7 %fusion.1 = f32[96,4,48]{2,1,0:T(4,128)S(1)} fusion(f32[96,4,48,768]{3,2,1,0:T(8,128)} %get-tuple-element.6, f32[96,4,48]{2,1,0:T(4,128)S(1)} %broadcast_maximum_fusion, f32[4,48,768]{2,1,0:T(8,128)S(1)} %convert_element_type.41, pred[96,768]{1,0:T(8,128)(4,1)S(1)} %compare_and_fusion), kind=kLoop, calls=%fused_computation.3 | loop fusion | flops 56604672 | bytes 57434112 | tf_op jit(solution)/shard_map/reduce_sum | solution.py:64
  316.8 24.2 %copy.33 = bf16[768,96,128]{0,2,1:T(8,128)(2,1)} copy(bf16[768,96,128]{2,1,0:T(8,128)(2,1)} %all-gather.5.cloned.1.call-done) | data formatting | bytes 37748736 | tf_op jit(solution)/shard_map/all_gather | solution.py:54
  341.0 29.1 %bitcast_divide_fusion = f32[48,96,4,32]{0,3,2,1:T(8,128)} fusion(f32[48,96,4]{0,2,1:T(4,128)S(1)} %bitcast.46, bf16[768,96,4,32]{0,3,2,1:T(8,128)(2,1)} %bitcast.42, f32[96,4,48,768]{3,2,1,0:T(8,128)} %get-tuple-element.6, f32[96,4,48]{2,1,0:T(4,128)S(1)} %broadcast_maximum_fusion, f32[4,48,768]{2,1,0:T(8,128)S(1)} %convert_element_type.41, ...), kind=kOutput, calls=%fused_computation.10 | convolution fusion | flops 963182592 | bytes 78667776 | tf_op jit(solution)/shard_map/jhik,kjhd->jhid/dot_general | solution.py:65
  370.1 6.6 %copy.34 = f32[48,96,4,32]{1,0,3,2:T(8,128)} copy(f32[48,96,4,32]{0,3,2,1:T(8,128)} %bitcast_divide_fusion) | data formatting | bytes 4718592 | tf_op jit(solution)/shard_map/div | solution.py:71
  376.7 4.2 %reshape.90 = f32[4608,128]{0,1:T(8,128)} reshape(f32[48,96,4,32]{1,0,3,2:T(8,128)} %copy.34) | data formatting | bytes 4718592 | tf_op jit(solution)/shard_map/reshape | solution.py:72
  380.9 3.1 copy.35
  383.9 3.6 convolution_convert_fusion
  (29 shorter events, 0.2 us)
Async XLA Ops:
  7.4 31.6 %copy-start = (bf16[128,128]{1,0:T(8,128)(2,1)S(1)}, bf16[128,128]{1,0:T(8,128)(2,1)}, u32[]{:S(2)}) copy-start(bf16[128,128]{1,0:T(8,128)(2,1)} %param.13) | copy-start | bytes 98308
  7.4 4.6 %copy-start.2 = (bf16[48,96,128]{2,1,0:T(8,128)(2,1)S(1)}, bf16[48,96,128]{2,1,0:T(8,128)(2,1)}, u32[]{:S(2)}) copy-start(bf16[48,96,128]{2,1,0:T(8,128)(2,1)} %param.9) | copy-start | bytes 3538948
  7.4 238.1 %all-reduce.2.cloned.1.call-start = ((), (), s32[]{:S(2)}) async-start(), calls=%async_computation.1 | async-start | bytes 589824 | tf_op jit(solution)/shard_map/psum | solution.py:11
  7.4 6.1 %copy-start.7 = (bf16[128,4]{0,1:T(4,128)(2,1)S(1)}, bf16[128,4]{0,1:T(4,128)(2,1)}, u32[]{:S(2)}) copy-start(bf16[128,4]{0,1:T(4,128)(2,1)} %param.16) | copy-start | bytes 3076
  38.2 2.5 copy-start.3
  38.9 207.6 %all-gather.3.cloned.1.call-start = ((), (), s32[]{:S(2)}) async-start(), calls=%async_computation | async-start | bytes 20054016 | tf_op jit(solution)/shard_map/all_gather | solution.py:50
  40.5 1.6 copy-start.4
  40.6 276.3 %all-gather.5.cloned.1.call-start = ((), (), s32[]{:S(2)}) async-start(), calls=%async_computation.2 | async-start | bytes 20054016 | tf_op jit(solution)/shard_map/all_gather | solution.py:54
  47.1 5.2 %copy-start.5 = (s32[768]{0:T(1024)S(1)}, s32[768]{0:T(1024)}, u32[]{:S(2)}) copy-start(s32[768]{0:T(1024)} %param.11) | copy-start | bytes 9220
  47.1 5.3 %copy-start.6 = (s32[768]{0:T(1024)S(1)}, s32[768]{0:T(1024)}, u32[]{:S(2)}) copy-start(s32[768]{0:T(1024)} %param.10) | copy-start | bytes 9220
  380.9 3.1 copy-start.8
  380.9 3.1 copy-start.9
  383.9 3.6 copy-start.1
Sparse Core Ops, SparseCore 0:
  39.1 206.3 all-reduce.1
Sparse Core Ops, SparseCore 1:
  41.2 105.0 all-gather.2
  148.0 107.0 all-gather.4
where the time goes:
time: 397 us; the launch traced here: 395 us
  waiting for transfers between devices  193 us (49%)
  local copies, waits for them, and re-layouts  73.1 us (18%)
  matrix products  62.9 us (16%)
  other arithmetic  27.6 us (7%)
  blocking collectives  23.1 us (6%)
  between operations  15 us (4%)
    psum x1, waiting for transfers between devices, from_root(): return lax.psum(block, axis)  193 us
    dot_general x1, matrix products, body(): jnp.einsum('jhik,kjhd->jhid', weights.astype(jnp.bfloat16), value_heads,...  29.1 us
    dot_general x1, matrix products, body(): jnp.einsum('ijhd,kjhd->jhik', query, key_heads, preferred_element_type=jn...  26.4 us
    all_gather x1, local copies, waits for them, and re-layouts, body(): key_piece = lax.all_gather(key_tile, 'row', axis=0, tiled=True)  24.2 us
    all_gather x1, local copies, waits for them, and re-layouts, body(): lax.all_gather(value_tile, 'row', axis=0, tiled=True)  24.2 us
    all_gather x1, blocking collectives, body(): bias_rows = lax.all_gather(bias_tile, 'row', axis=1, tiled=True)  23.1 us
    reduce_sum x1, other arithmetic, body(): new_total = jnp.sum(weights, axis=-1)  19.7 us
    reshape x2, local copies, waits for them, and re-layouts, body(): query = project(flat, w_query, factor).reshape(rows, cols, heads, head_dim)  8.06 us
  transfers between devices with their start and end apart: 3, of which 1 were waited for; matrix products, arithmetic and copies ran while one was open for 21% of the time, Pallas kernels for 0%

commit v1 on v0

v1 whole, which is shorter than its diff:
```python
import functools
import math

import jax
import jax.numpy as jnp
from jax import lax
from jax.experimental import pallas as pl
from jax.experimental.pallas import tpu as pltpu
from jax.sharding import PartitionSpec as P

LOG2E = math.log2(math.e)
NT = (((1,), (1,)), ((), ()))
NEG = -1e30


def normalize(pair):
    values = pair.astype(jnp.float32)
    center = jnp.mean(values, axis=-1, keepdims=True)
    spread = jnp.mean((values - center) ** 2, axis=-1, keepdims=True)
    return ((values - center) * lax.rsqrt(spread + 1e-05)).astype(jnp.bfloat16)


def attend(heads, x_ref, bias_ref, mask_ref, wqg_ref, wkt_ref, wv_ref, wo_ref, out_ref, kt, va, q_s, g_s, acc):
    ncol, count, width = x_ref.shape
    head_dim = width // heads
    lane = lax.broadcasted_iota(jnp.int32, (count, width), 1) // head_dim
    kt[...] = jnp.zeros_like(kt)
    va[:, width:] = jnp.ones((count, width), jnp.bfloat16)
    q_s[:, width:] = (lax.broadcasted_iota(jnp.int32, (count, width), 1) == 0).astype(jnp.bfloat16)

    def column(j, _):
        x = x_ref[j]
        qg = jnp.dot(x, wqg_ref[...], preferred_element_type=jnp.float32)
        q = qg[:, :width] * (LOG2E / math.sqrt(head_dim))
        g_s[...] = jax.nn.sigmoid(qg[:, width:])
        kt[:width, :] = lax.dot_general(wkt_ref[...], x, NT, preferred_element_type=jnp.float32).astype(jnp.bfloat16)
        first = lax.broadcasted_iota(jnp.int32, (16, count), 0) == 0
        kt[width : width + 16, :] = jnp.where(first, mask_ref[pl.ds(j, 1), :], 0.0).astype(jnp.bfloat16)
        va[:, :width] = jnp.dot(x, wv_ref[...], preferred_element_type=jnp.float32).astype(jnp.bfloat16)
        for h in range(heads):
            q_s[:, :width] = jnp.where(lane == h, q, 0.0).astype(jnp.bfloat16)
            s = jnp.dot(q_s[...], kt[...], preferred_element_type=jnp.float32)
            s = s + bias_ref[h].astype(jnp.float32) * LOG2E
            peak = jnp.max(s, axis=1, keepdims=True)
            p = jnp.exp2(s - peak).astype(jnp.bfloat16)
            o = jnp.dot(p, va[...], preferred_element_type=jnp.float32)
            acc[...] = o if h == 0 else jnp.where(jnp.concatenate([lane, lane], 1) == h, o, acc[...])
        o = acc[...]
        gated = (o[:, :width] / o[:, width:] * g_s[...]).astype(jnp.bfloat16)
        out_ref[j] = jnp.dot(gated, wo_ref[...], preferred_element_type=jnp.float32).astype(jnp.bfloat16)
        return 0

    lax.fori_loop(0, ncol, column, 0)


def attention(heads, x, bias, mask, wqg, wkt, wv, wo):
    ncol, count, width = x.shape
    return pl.pallas_call(
        functools.partial(attend, heads),
        out_shape=jax.ShapeDtypeStruct(x.shape, jnp.bfloat16),
        in_specs=[pl.BlockSpec(memory_space=pltpu.VMEM)] * 7,
        out_specs=pl.BlockSpec(memory_space=pltpu.VMEM),
        scratch_shapes=[
            pltpu.VMEM((2 * width, count), jnp.bfloat16),
            pltpu.VMEM((count, 2 * width), jnp.bfloat16),
            pltpu.VMEM((count, 2 * width), jnp.bfloat16),
            pltpu.VMEM((count, width), jnp.float32),
            pltpu.VMEM((count, 2 * width), jnp.float32),
        ],
        compiler_params=pltpu.CompilerParams(vmem_limit_bytes=52 * 2**20),
    )(x, bias, mask, wqg, wkt, wv, wo)


def body(pair, token_mask, chain_ids, w_query, w_key, w_value, w_gate, w_bias, w_out):
    rows, cols, width = pair.shape
    heads = w_bias.shape[1]
    count = token_mask.shape[0]
    members = count // rows
    mine = cols // members
    normed = jnp.swapaxes(normalize(pair), 0, 1)
    x = lax.all_to_all(normed, "row", 0, 1, tiled=True)
    first = lax.axis_index("col") * cols + lax.axis_index("row") * mine
    bias = lax.dot_general(w_bias, x, (((0,), (2,)), ((), ())), preferred_element_type=jnp.float32).astype(jnp.bfloat16)
    bias = lax.all_gather(bias, ("col", "row"), axis=1, tiled=True)
    my_chain = lax.dynamic_slice_in_dim(chain_ids, first, mine)
    keep = (token_mask == 1)[None, :] & (chain_ids[None, :] == my_chain[:, None])
    mask = jnp.where(keep, 0.0, NEG).astype(jnp.float32)
    update = attention(heads, x, bias, mask, jnp.concatenate([w_query, w_gate], 1), w_key.T, w_value, w_out)
    update = lax.all_to_all(update, "row", 1, 0, tiled=True)
    return jnp.swapaxes(update, 0, 1)


def solution(mesh):
    placed = (P("row", "col", None), P(), P(), P(), P(), P(), P(), P(), P())
    return jax.shard_map(
        body, mesh=mesh, in_specs=placed, out_specs=P("row", "col", None), check_vma=False
    )
```

time: 397 us -> 172 us (0.43)
  the two profiles are of different devices: /device:TPU:6 before, /device:TPU:1 now
where the time goes in v1:
time: 172 us; the launch traced here: 171 us
  waiting for transfers between devices  66.4 us (39%)
  blocking collectives  49 us (28%)
  Pallas kernels  27.2 us (16%)
  between operations  13.6 us (8%)
  local copies, waits for them, and re-layouts  7.72 us (4%)
  other arithmetic  6.43 us (4%)
    all_gather x1, waiting for transfers between devices, body(): bias = lax.all_gather(bias, ('col', 'row'), axis=1, tiled=True)  66.4 us
    pallas_call x1, Pallas kernels, attention(): pl.pallas_call(functools.partial(attend, heads), out_shape=jax.ShapeDtype...  27.2 us
    all_to_all x1, blocking collectives, body(): x = lax.all_to_all(normed, 'row', 0, 1, tiled=True)  25 us
    all_to_all x1, blocking collectives, body(): update = lax.all_to_all(update, 'row', 1, 0, tiled=True)  24 us
    all_gather x1, local copies, waits for them, and re-layouts, body(): bias = lax.all_gather(bias, ('col', 'row'), axis=1, tiled=True)  5.1 us
  transfers between devices with their start and end apart: 1, of which 1 were waited for; matrix products, arithmetic and copies ran while one was open for 0% of the time, Pallas kernels for 0%

profile of v1, /device:TPU:1, one launch (start us, length us, event | category | flops | bytes accessed | tf_op | source)
XLA Modules:
  0.0 171.4 jit_solution(16491982855897276303)
XLA Ops:
  6.5 0.0 copy-start
  6.5 0.0 all-gather.2.cloned.1.call-start
  6.5 2.1 %convert_reduce_fusion = f32[48,96]{0,1:T(8,128)S(1)} fusion(bf16[48,96,128]{2,1,0:T(8,128)(2,1)} %param.9), kind=kLoop, calls=%fused_computation.1 | loop fusion | flops 1175040 | bytes 1198080 | tf_op jit(solution)/shard_map/reduce_sum | solution.py:18
  8.6 0.0 copy-done.3
  8.6 2.3 %fusion.2 = f32[48,96]{0,1:T(8,128)S(1)} fusion(f32[48,96]{0,1:T(8,128)S(1)} %broadcast_multiply_fusion, bf16[48,96,128]{2,1,0:T(8,128)(2,1)S(1)} %copy-done.3), kind=kLoop, calls=%fused_computation.4 | loop fusion | flops 2354688 | bytes 1216512 | tf_op jit(solution)/shard_map/reduce_sum | solution.py:19
  10.9 2.0 %fusion.4 = bf16[96,48,128]{2,1,0:T(8,128)(2,1)S(1)} fusion(f32[48,96]{0,1:T(8,128)S(1)} %add_rsqrt_fusion, f32[48,96]{0,1:T(8,128)S(1)} %broadcast_multiply_fusion, bf16[48,96,128]{2,1,0:T(8,128)(2,1)S(1)} %copy-done.3), kind=kLoop, calls=%fused_computation.6 | loop fusion | flops 2359296 | bytes 2396160 | tf_op jit(solution)/shard_map/transpose | solution.py:80
  12.9 25.0 %all_to_all.36 = bf16[96,48,128]{2,1,0:T(8,128)(2,1)S(1)} all-to-all(bf16[96,48,128]{2,1,0:T(8,128)(2,1)S(1)} %fusion.4), channel_id=1, replica_groups=mesh['row'=16,'col'=8] {'row'}, dimensions={0} | all-to-all | bytes 2359296 | tf_op jit(solution)/shard_map/all_to_all | solution.py:81
  38.0 0.1 copy.27
  38.0 0.0 copy-start.4
  38.0 0.0 copy-start.5
  38.1 0.0 copy-start.9
  38.1 0.0 copy-start.6
  38.1 0.0 copy-start.7
  38.1 0.0 copy-start.8
  38.1 0.0 copy-done
  38.1 1.0 fusion.5
  39.2 0.0 all-gather.2.cloned.1.call-update
  39.2 0.0 copy-done.5
  39.2 0.1 copy.28
  39.3 0.0 copy-done.9
  39.3 0.1 dynamic_slice.3
  39.4 0.0 copy-done.6
  39.4 0.0 copy-done.7
  39.4 0.0 copy-done.8
  39.4 0.1 and_select_fusion.mask_ref
  39.5 66.4 %all-gather.2.cloned.1.call-done = bf16[4,768,768]{2,0,1:T(4,128)(2,1)} async-done(((bf16[4,6,768]{2,0,1:T(4,128)(2,1)}), bf16[4,768,768]{2,0,1:T(4,128)(2,1)}) %all-gather.2.cloned.1.call-update) | async-done | bytes 4718608 | tf_op jit(solution)/shard_map/all_gather | solution.py:84
  105.9 5.1 %copy.29.bias_ref = bf16[4,768,768]{2,1,0:T(8,128)(2,1)} copy(bf16[4,768,768]{2,0,1:T(4,128)(2,1)} %all-gather.2.cloned.1.call-done) | data formatting | bytes 9437184 | tf_op jit(solution)/shard_map/all_gather | solution.py:84
  111.0 27.2 %shard_map.91 = bf16[6,768,128]{2,1,0:T(8,128)(2,1)S(1)} custom-call(bf16[6,768,128]{2,1,0:T(8,128)(2,1)} %bitcast.21, bf16[4,768,768]{2,1,0:T(8,128)(2,1)} %copy.29.bias_ref, f32[6,768]{1,0:T(8,128)S(1)} %and_select_fusion.mask_ref, bf16[128,256]{1,0:T(8,128)(2,1)S(1)} %pad_maximum_fusion.wqg_ref, bf16[128,128]{1,0:T(8,128)(2,1)S(1)} %bitcast.19, ...), custom_call_target="tpu_custom_call" | custom-call | tf_op jit(solution)/shard_map/pallas_call | solution.py:58
  138.2 0.8 copy.30
  139.1 24.0 %all_to_all.37 = bf16[6,768,128]{2,0,1:T(8,128)(2,1)S(1)} all-to-all(bf16[6,768,128]{2,0,1:T(8,128)(2,1)S(1)} %copy.30), channel_id=1, replica_groups=mesh['row'=16,'col'=8] {'row'}, dimensions={1} | all-to-all | bytes 2359296 | tf_op jit(solution)/shard_map/all_to_all | solution.py:89
  163.1 0.2 copy.32
  163.2 1.3 copy.33
  (10 shorter events, 0.0 us)
Async XLA Ops:
  6.5 31.6 %copy-start = (bf16[128,4]{0,1:T(4,128)(2,1)S(1)}, bf16[128,4]{0,1:T(4,128)(2,1)}, u32[]{:S(2)}) copy-start(bf16[128,4]{0,1:T(4,128)(2,1)} %param.16) | copy-start | bytes 3076
  6.5 2.1 %copy-start.3 = (bf16[48,96,128]{2,1,0:T(8,128)(2,1)S(1)}, bf16[48,96,128]{2,1,0:T(8,128)(2,1)}, u32[]{:S(2)}) copy-start(bf16[48,96,128]{2,1,0:T(8,128)(2,1)} %param.9) | copy-start | bytes 3538948
  6.5 99.3 %all-gather.2.cloned.1.call-start = ((), (), s32[]{:S(2)}) async-start(), calls=%async_computation.2 | async-start | bytes 4755456 | tf_op jit(solution)/shard_map/all_gather | solution.py:84
  38.0 73.0 %copy-start.4 = (bf16[6,16,48,128]{3,2,1,0:T(8,128)(2,1)}, bf16[6,16,48,128]{3,2,1,0:T(8,128)(2,1)S(1)}, u32[]{:S(2)}) copy-start(bf16[6,16,48,128]{3,2,1,0:T(8,128)(2,1)S(1)} %copy.27) | copy-start | bytes 3538948
  38.0 1.1 copy-start.5
  38.1 1.2 copy-start.9
  38.1 1.3 copy-start.6
  38.1 1.3 copy-start.7
  38.1 1.3 copy-start.8
  39.5 71.5 %copy-start.1 = (bf16[128,128]{1,0:T(8,128)(2,1)S(1)}, bf16[128,128]{1,0:T(8,128)(2,1)}, u32[]{:S(2)}) copy-start(bf16[128,128]{1,0:T(8,128)(2,1)} %wv_ref.1) | copy-start | bytes 98308
  39.5 71.5 %copy-start.2 = (bf16[128,128]{1,0:T(8,128)(2,1)S(1)}, bf16[128,128]{1,0:T(8,128)(2,1)}, u32[]{:S(2)}) copy-start(bf16[128,128]{1,0:T(8,128)(2,1)} %wo_ref.1) | copy-start | bytes 98308
Sparse Core Ops, SparseCore 0:
  39.3 66.5 all-gather.1

commit v2 on v1

v2 whole, which is shorter than its diff:
```python
import functools
import math

import jax
import jax.numpy as jnp
from jax import lax
from jax.experimental import pallas as pl
from jax.experimental.pallas import tpu as pltpu
from jax.sharding import PartitionSpec as P

LOG2E = math.log2(math.e)
NT = (((1,), (1,)), ((), ()))
NEG = -1e30
MESH = pl.DeviceIdType.MESH
Z, X, Y = 4, 4, 4
GROUP = 3


def kernel(
    heads,
    pair_ref, mask_ref, wqg_ref, wkt_ref, wv_ref, wbt_ref, wo_ref, out_ref,
    normed, bias_f32, sent, x_ref, tiles, bias, q_s, g_s, kt, va, acc, back,
    in_send, in_recv, z_send, z_recv, y_send, y_recv, x1_send, x1_recv, x2_send, x2_recv,
    sib_send, sib_recv, out_send, out_recv,
):
    rows, cols, width = pair_ref.shape
    ncol, count, _ = x_ref.shape
    head_dim = width // heads
    members = count // rows
    half = count // 2
    row, col = lax.axis_index("row"), lax.axis_index("col")
    core, z, y_lo = lax.rem(row, 2), lax.rem(row // 2, Z), row // (2 * Z)
    x, y_hi = col // 2, lax.rem(col, 2)
    y = y_hi * 2 + y_lo
    place = row // 2
    slot = core * (members // 2) + place
    sibling = (row + 1 - 2 * core, col)
    right, left = (row, lax.rem(x + 1, X) * 2 + y_hi), (row, lax.rem(x + X - 1, X) * 2 + y_hi)
    x_left, x_right, x_far = lax.rem(x + X - 1, X), lax.rem(x + 1, X), lax.rem(x + 2, X)

    def y_peer(step):
        there = lax.rem(y + step, Y)
        return ((lax.rem(there, 2) * Z + z) * 2 + core, x * 2 + there // 2)

    def send(src, dst, send_sem, recv_sem, device):
        pltpu.make_async_remote_copy(
            src_ref=src, dst_ref=dst, send_sem=send_sem, recv_sem=recv_sem, device_id=device, device_id_type=MESH
        ).start()

    def await_bytes(ref, sem):
        pltpu.make_async_copy(ref, ref, sem).wait()

    barrier = pltpu.get_barrier_semaphore()

    def greet(step, _):
        pl.semaphore_signal(barrier, inc=1, device_id=(lax.rem(row + step, members), col), device_id_type=MESH)
        return 0

    lax.fori_loop(1, members, greet, 0)
    for device in (right, left, y_peer(2), y_peer(3 - 2 * y_lo)):
        pl.semaphore_signal(barrier, inc=1, device_id=device, device_id_type=MESH)

    bias_f32[...] = jnp.zeros_like(bias_f32)
    many = 4

    def norm(t, _):
        values = pair_ref[pl.ds(t * many, many)].reshape(many * cols, width).astype(jnp.float32)
        center = jnp.mean(values, axis=-1, keepdims=True)
        spread = jnp.mean((values - center) ** 2, axis=-1, keepdims=True)
        block = ((values - center) * lax.rsqrt(spread + 1e-05)).astype(jnp.bfloat16)
        normed[pl.ds(pl.multiple_of(t * many * cols, many * cols), many * cols), :] = block.astype(jnp.float32)
        for u in range(many):
            part = block[u * cols : (u + 1) * cols]
            line = lax.dot_general(wbt_ref[...], part, NT, preferred_element_type=jnp.float32)
            bias_f32[pl.ds(pl.multiple_of((t * many + u) * 8, 8), 8), :cols] = line[:8]
        return 0

    lax.fori_loop(0, rows // many, norm, 0)
    mine = pl.ds(pl.multiple_of(place * rows, rows), rows)
    for h in range(heads):
        tiles[h, y_hi, mine, :] = bias_f32[pl.ds(h, rows, stride=8), :].astype(jnp.bfloat16)

    pl.semaphore_wait(barrier, members + 3)
    for step in range(1, Z):
        there = (row - 2 * z + 2 * lax.rem(z + step, Z), col)
        send(tiles.at[:, y_hi, mine], tiles.at[:, y_hi, mine], z_send, z_recv, there)

    def turn(t, _):
        for u in range(many):
            j = t * many + u
            sent[j] = normed[pl.ds(j, rows, stride=cols), :].astype(jnp.bfloat16)
        return 0

    lax.fori_loop(0, cols // many, turn, 0)
    here = pl.ds(pl.multiple_of(slot * rows, rows), rows)
    for g in range(ncol // GROUP):
        def scatter(step, _, g=g):
            peer = lax.rem(row + step, members)
            send(
                sent.at[pl.ds(peer * ncol + g * GROUP, GROUP)],
                x_ref.at[pl.ds(g * GROUP, GROUP), here],
                in_send, in_recv.at[g], (peer, col),
            )
            return 0

        lax.fori_loop(1, members, scatter, 0)
    for j in range(ncol):
        x_ref[j, here, :] = sent[row * ncol + j]

    await_bytes(tiles.at[:, 0, pl.ds(0, (Z - 1) * rows)], z_recv)
    quarter = pl.ds(pl.multiple_of(y_lo * Z * rows, Z * rows), Z * rows)
    for h in range(heads):
        for step in range(1, Y):
            block = tiles.at[h, y_hi, quarter]
            send(block, block, y_send, y_recv.at[h, step - 1], y_peer(step))

    wide = cols // 2
    eye = (
        lax.broadcasted_iota(jnp.int32, (cols, 128), 0) == lax.broadcasted_iota(jnp.int32, (cols, 128), 1)
    ).astype(jnp.bfloat16)

    def owned(h, owner, part=slice(None)):
        return bias.at[h, core, part, pl.ds(pl.multiple_of(owner * cols, cols), cols)]

    for h in range(heads):
        for step in range(1, Y):
            await_bytes(tiles.at[h, 0, pl.ds(0, Z * rows)], y_recv.at[h, step - 1])
        for side in range(2):
            turned = lax.dot_general(eye, tiles[h, side], NT, preferred_element_type=jnp.float32).astype(jnp.bfloat16)
            for part in range(2):
                at = pl.ds(pl.multiple_of(x * cols + side * wide, wide), wide)
                bias[h, core, part, at, :] = turned[part * wide : (part + 1) * wide]
        block = owned(h, x)
        send(block, block, x1_send, x1_recv.at[h, 0], right)
        send(block, block, x1_send, x1_recv.at[h, 1], left)
        send(block, block, sib_send, sib_recv.at[h, 0], sibling)

    def forward(h):
        await_bytes(owned(h, x_left), x1_recv.at[h, 0])
        block = owned(h, x_left, 0)
        send(block, block, x2_send, x2_recv.at[h, 0], right)
        block = owned(h, x_left)
        send(block, block, sib_send, sib_recv.at[h, 1], sibling)
        await_bytes(owned(h, x_right), x1_recv.at[h, 1])
        block = owned(h, x_right, 1)
        send(block, block, x2_send, x2_recv.at[h, 1], left)
        block = owned(h, x_right)
        send(block, block, sib_send, sib_recv.at[h, 2], sibling)

    def pass_on(h):
        for part in range(2):
            block = owned(h, x_far, part)
            await_bytes(block, x2_recv.at[h, part])
            send(block, block, sib_send, sib_recv.at[h, 3 + part], sibling)

    def complete(h):
        for n in range(3):
            await_bytes(owned(h, x), sib_recv.at[h, n])
        for n in range(2):
            await_bytes(owned(h, x, 0), sib_recv.at[h, 3 + n])

    lane = lax.broadcasted_iota(jnp.int32, (count, width), 1) // head_dim
    one = (lax.broadcasted_iota(jnp.int32, (count, width), 1) == 0).astype(jnp.bfloat16)

    def project(j, _):
        block = x_ref[j]
        qg = jnp.dot(block, wqg_ref[...], preferred_element_type=jnp.float32)
        q_s[j] = (qg[:, :width] * (LOG2E / math.sqrt(head_dim))).astype(jnp.bfloat16)
        g_s[j] = jax.nn.sigmoid(qg[:, width:])
        kt[j, :width, :] = lax.dot_general(wkt_ref[...], block, NT, preferred_element_type=jnp.float32).astype(
            jnp.bfloat16
        )
        first = lax.broadcasted_iota(jnp.int32, (16, count), 0) == 0
        kt[j, width : width + 16, :] = jnp.where(first, mask_ref[pl.ds(j, 1), :], 0.0).astype(jnp.bfloat16)
        kt[j, width + 16 :, :] = jnp.zeros((width - 16, count), jnp.bfloat16)
        va[j, :, :width] = jnp.dot(block, wv_ref[...], preferred_element_type=jnp.float32).astype(jnp.bfloat16)
        va[j, :, width:] = jnp.ones((count, width), jnp.bfloat16)
        return 0

    for g in range(ncol // GROUP):
        await_bytes(x_ref.at[pl.ds(0, GROUP), pl.ds(0, count - rows)], in_recv.at[g])
        lax.fori_loop(g * GROUP, (g + 1) * GROUP, project, 0)
        if g == 0:
            forward(0)

    def attend(h, j):
        q = jnp.where(lane == h, q_s[j], jnp.zeros((count, width), jnp.bfloat16))
        s = jnp.dot(jnp.concatenate([q, one], 1), kt[j], preferred_element_type=jnp.float32)
        b = jnp.concatenate([bias[h, n].reshape(count, half) for n in range(2)], 1)
        s = s + b.astype(jnp.float32) * LOG2E
        peak = jnp.max(s, axis=1, keepdims=True)
        p = jnp.exp2(s - peak).astype(jnp.bfloat16)
        o = jnp.dot(p, va[j], preferred_element_type=jnp.float32)
        acc[j] = o if h == 0 else jnp.where(jnp.concatenate([lane, lane], 1) == h, o, acc[j])

    def only(h):
        def step(j, _):
            attend(h, j)
            return 0
        return step

    def last(j, _):
        attend(heads - 2, j)
        attend(heads - 1, j)
        o = acc[j]
        gated = (o[:, :width] / o[:, width:] * g_s[j]).astype(jnp.bfloat16)
        back[j] = jnp.dot(gated, wo_ref[...], preferred_element_type=jnp.float32).astype(jnp.bfloat16)

        def give(step, _):
            peer = lax.rem(row + step, members)
            at = (lax.rem(peer, 2) * (members // 2) + peer // 2) * rows
            send(
                back.at[j, pl.ds(pl.multiple_of(at, rows), rows)], out_ref.at[row * ncol + j],
                out_send, out_recv, (peer, col),
            )
            return 0

        lax.fori_loop(1, members, give, 0)
        out_ref[row * ncol + j] = back[j, here, :]
        return 0

    pass_on(0)
    forward(1)
    complete(0)
    lax.fori_loop(0, ncol // 2, only(0), 0)
    pass_on(1)
    forward(2)
    lax.fori_loop(ncol // 2, ncol, only(0), 0)
    complete(1)
    lax.fori_loop(0, ncol // 2, only(1), 0)
    pass_on(2)
    forward(3)
    lax.fori_loop(ncol // 2, ncol, only(1), 0)
    pass_on(3)
    complete(2)
    complete(3)
    lax.fori_loop(0, ncol, last, 0)

    await_bytes(out_ref.at[pl.ds(0, (members - 1) * ncol)], out_recv)
    await_bytes(out_ref.at[pl.ds(0, (members - 1) * ncol)], out_send)
    await_bytes(sent.at[pl.ds(0, (members - 1) * ncol)], in_send)
    await_bytes(tiles.at[:, 0, pl.ds(0, (Z - 1) * rows)], z_send)
    await_bytes(tiles.at[pl.ds(0, Y - 1)], y_send)
    await_bytes(bias.at[0], x1_send)
    await_bytes(bias.at[0, 0], x2_send)
    await_bytes(bias.at[:, 0], sib_send)


def exchange(heads, ncol, count, pair, mask, wqg, wkt, wv, wbt, wo):
    rows, cols, width = pair.shape
    half = count // 2
    bf16, f32 = jnp.bfloat16, jnp.float32
    dma = pltpu.SemaphoreType.DMA
    return pl.pallas_call(
        functools.partial(kernel, heads),
        out_shape=jax.ShapeDtypeStruct((cols, rows, width), bf16),
        in_specs=[pl.BlockSpec(memory_space=pltpu.VMEM)] * 7,
        out_specs=pl.BlockSpec(memory_space=pltpu.VMEM),
        scratch_shapes=[
            pltpu.VMEM((rows * cols, width), f32),
            pltpu.VMEM((rows * 8, 128), f32),
            pltpu.VMEM((cols, rows, width), bf16),
            pltpu.VMEM((ncol, count, width), bf16),
            pltpu.VMEM((heads, 2, half, 128), bf16),
            pltpu.VMEM((heads, 2, 2, half, half), bf16),
            pltpu.VMEM((ncol, count, width), bf16),
            pltpu.VMEM((ncol, count, width), f32),
            pltpu.VMEM((ncol, 2 * width, count), bf16),
            pltpu.VMEM((ncol, count, 2 * width), bf16),
            pltpu.VMEM((ncol, count, 2 * width), f32),
            pltpu.VMEM((ncol, count, width), bf16),
            dma, dma((ncol // GROUP,)), dma, dma, dma, dma((heads, Y - 1)), dma, dma((heads, 2)), dma, dma((heads, 2)),
            dma, dma((heads, 5)), dma, dma,
        ],
        compiler_params=pltpu.CompilerParams(
            collective_id=0, has_side_effects=True, vmem_limit_bytes=56 * 2**20
        ),
        cost_estimate=pl.CostEstimate(flops=4 * 10**9, bytes_accessed=10**7, transcendentals=15 * 10**6),
    )(pair, mask, wqg, wkt, wv, wbt, wo)


def body(pair, token_mask, chain_ids, w_query, w_key, w_value, w_gate, w_bias, w_out):
    rows, cols, width = pair.shape
    heads = w_bias.shape[1]
    count = token_mask.shape[0]
    members = count // rows
    ncol = cols // members
    first = lax.axis_index("col") * cols + lax.axis_index("row") * ncol

    def order(tokens):
        return tokens.reshape(members // 2, 2, rows).swapaxes(0, 1).reshape(count)

    my_chain = lax.dynamic_slice_in_dim(chain_ids, first, ncol)
    keep = (order(token_mask) == 1)[None, :] & (order(chain_ids)[None, :] == my_chain[:, None])
    mask = jnp.where(keep, 0.0, NEG).astype(jnp.float32)
    wbt = jnp.pad(w_bias.T, ((0, 16 - heads), (0, 0)))
    wqg = jnp.concatenate([w_query, w_gate], 1)
    update = exchange(heads, ncol, count, pair, mask, wqg, w_key.T, w_value, wbt, w_out)
    return jnp.swapaxes(update, 0, 1)


def solution(mesh):
    placed = (P("row", "col", None), P(), P(), P(), P(), P(), P(), P(), P())
    return jax.shard_map(
        body, mesh=mesh, in_specs=placed, out_specs=P("row", "col", None), check_vma=False
    )
```

time: 172 us -> 99.1 us (0.58)
  waiting for transfers between devices: 66.4 us -> 0 us
  Pallas kernels: 27.2 us -> 88.8 us
  blocking collectives: 49 us -> 0 us
  between operations: 13.6 us -> 0.03 us
  other arithmetic: 6.43 us -> 2.78 us
    all_gather x1 -> x0, waiting for transfers between devices: 66.4 us -> none  [body(): bias = lax.all_gather(bias, ('col', 'row'), axis=1, tiled=True)]
    pallas_call x1, Pallas kernels: 27.2 us -> 88.8 us  [exchange(): pl.pallas_call(functools.partial(kernel, heads), out_shape=jax.ShapeDtype...]
    all_to_all x2 -> x0, blocking collectives: 49 us -> none  [the longest x1 25 us: body(): x = lax.all_to_all(normed, 'row', 0, 1, tiled=True)]
    all_gather x1 -> x0, local copies, waits for them, and re-layouts: 5.1 us -> none  [body(): bias = lax.all_gather(bias, ('col', 'row'), axis=1, tiled=True)]
    reduce_sum x2 -> x0, other arithmetic: 4.32 us -> none  [the longest x1 2.26 us: normalize(): spread = jnp.mean((values - center) ** 2, axis=-1, keepdims=True)]
    transpose x1 -> x0, other arithmetic: 2 us -> none  [body(): normed = jnp.swapaxes(normalize(pair), 0, 1)]
  transfers between devices with their start and end apart: 1 -> 0, of which waited for: 1 -> 0; matrix products, arithmetic and copies ran while one was open for 0% -> 0% of each run, Pallas kernels for 0% -> 0%
where the time goes in v2:
time: 99.1 us; the launch traced here: 98.7 us
  Pallas kernels  88.8 us (90%)
  local copies, waits for them, and re-layouts  7.12 us (7%)
  other arithmetic  2.78 us (3%)
    pallas_call x1, Pallas kernels, exchange(): pl.pallas_call(functools.partial(kernel, heads), out_shape=jax.ShapeDtype...  88.8 us
    transpose x1, local copies, waits for them, and re-layouts, body(): return jnp.swapaxes(update, 0, 1)  2.59 us

profile of v2, /device:TPU:1, one launch (start us, length us, event | category | flops | bytes accessed | tf_op | source)
XLA Modules:
  0.0 98.7 jit_solution(12340057467325114736)
XLA Ops:
  0.0 0.8 dynamic_slice.3
  0.8 0.7 broadcast_compare_fusion
  1.5 0.1 eq.36
  1.6 0.1 eq.38
  1.6 1.3 %pad.4.wbt_ref = bf16[16,128]{1,0:T(8,128)(2,1)} pad(bf16[4,128]{1,0:T(4,128)(2,1)} %bitcast.9, bf16[]{:T(256)} %constant.24.clone.1), padding=0_12x0_0 | pad | bytes 5122 | tf_op jit(solution)/shard_map/jit(_pad)/pad | solution.py:296
  2.9 0.8 reshape.16
  3.7 0.1 eq.39
  3.8 0.7 and_select_fusion.mask_ref
  4.5 1.5 %copy.17 = bf16[128,128]{0,1:T(8,128)(2,1)} copy(bf16[128,128]{1,0:T(8,128)(2,1)} %param.13) | data formatting | bytes 65536 | tf_op args[4]
  5.9 1.4 %pad_maximum_fusion.wqg_ref = bf16[128,256]{1,0:T(8,128)(2,1)} fusion(bf16[128,128]{1,0:T(8,128)(2,1)} %param.15, bf16[128,128]{1,0:T(8,128)(2,1)} %param.12), kind=kLoop, calls=%fused_computation | loop fusion | flops 131072 | bytes 131072 | tf_op jit(solution)/shard_map/concatenate | solution.py:297
  7.3 88.8 %shard_map.91 = bf16[96,48,128]{2,1,0:T(8,128)(2,1)} custom-call(bf16[48,96,128]{2,1,0:T(8,128)(2,1)} %pair_ref.1, f32[6,768]{1,0:T(8,128)} %and_select_fusion.mask_ref, bf16[128,256]{1,0:T(8,128)(2,1)} %pad_maximum_fusion.wqg_ref, bf16[128,128]{1,0:T(8,128)(2,1)} %bitcast.6, bf16[128,128]{1,0:T(8,128)(2,1)} %wv_ref.1, bf16[16,128]{1,0:T(8,128)(2,1)} %pad.4.wbt_ref, ...), custom_call_target="tpu_custom_call" | custom-call | flops 4000000000 | bytes 10000000 | tf_op jit(solution)/shard_map/pallas_call | solution.py:254
  96.1 2.6 %copy.18 = bf16[48,96,128]{2,1,0:T(8,128)(2,1)} copy(bf16[48,96,128]{2,0,1:T(8,128)(2,1)} %bitcast.5) | data formatting | bytes 2359296 | tf_op jit(solution)/shard_map/transpose | solution.py:299
  (2 shorter events, 0.0 us)

commit v3 on v2

v3 whole, which is shorter than its diff:
```python
import functools
import math

import jax
import jax.numpy as jnp
from jax import lax
from jax.experimental import pallas as pl
from jax.experimental.pallas import tpu as pltpu
from jax.sharding import PartitionSpec as P

LOG2E = math.log2(math.e)
NT = (((1,), (1,)), ((), ()))
NEG = -1e30
MESH = pl.DeviceIdType.MESH
Z, X = 4, 4
GROUP = 2


def kernel(
    heads,
    pair_ref, token_ref, chains_ref, chain_ref, wq_ref, wk_ref, wv_ref, wg_ref, wb_ref, wo_ref, out_ref,
    normed, bias_f32, sent, x_ref, tiles, bias, q_s, g_s, kt, va, acc, score, back,
    in_send, in_recv, t_send, t_recv, y_send, y_recv, x1_send, x1_recv, x2_send, x2_recv,
    sib_send, sib_recv, out_send, out_recv,
):
    rows, cols, width = pair_ref.shape
    ncol, count, _ = x_ref.shape
    head_dim = width // heads
    members = count // rows
    half = count // 2
    row, col = lax.axis_index("row"), lax.axis_index("col")
    core, z, y_lo = lax.rem(row, 2), lax.rem(row // 2, Z), row // (2 * Z)
    x, y_hi = col // 2, lax.rem(col, 2)
    y = y_hi * 2 + y_lo
    place = row // 2
    slot = core * (members // 2) + place
    sibling = (row + 1 - 2 * core, col)
    right, left = (row, lax.rem(x + 1, X) * 2 + y_hi), (row, lax.rem(x + X - 1, X) * 2 + y_hi)
    x_left, x_right, x_far = lax.rem(x + X - 1, X), lax.rem(x + 1, X), lax.rem(x + 2, X)

    there = lax.rem(y + 3 - 2 * y_lo, 4)
    across = ((lax.rem(there, 2) * Z + z) * 2 + core, x * 2 + there // 2)

    def send(src, dst, send_sem, recv_sem, device):
        pltpu.make_async_remote_copy(
            src_ref=src, dst_ref=dst, send_sem=send_sem, recv_sem=recv_sem, device_id=device, device_id_type=MESH
        ).start()

    def await_bytes(ref, sem):
        pltpu.make_async_copy(ref, ref, sem).wait()

    barrier = pltpu.get_barrier_semaphore()

    def greet(step, _):
        pl.semaphore_signal(barrier, inc=1, device_id=(lax.rem(row + step, members), col), device_id_type=MESH)
        return 0

    lax.fori_loop(1, members, greet, 0)
    for device in (right, left, across):
        pl.semaphore_signal(barrier, inc=1, device_id=device, device_id_type=MESH)

    bias_f32[...] = jnp.zeros_like(bias_f32)
    many = 4

    def norm(t, _):
        values = pair_ref[pl.ds(t * many, many)].reshape(many * cols, width).astype(jnp.float32)
        center = jnp.mean(values, axis=-1, keepdims=True)
        spread = jnp.mean((values - center) ** 2, axis=-1, keepdims=True)
        block = ((values - center) * lax.rsqrt(spread + 1e-05)).astype(jnp.bfloat16)
        normed[pl.ds(pl.multiple_of(t * many * cols, many * cols), many * cols), :] = block.astype(jnp.float32)
        for u in range(many):
            part = block[u * cols : (u + 1) * cols]
            line = lax.dot_general(wb_ref[...], part, NT, preferred_element_type=jnp.float32)
            bias_f32[pl.ds(pl.multiple_of((t * many + u) * 8, 8), heads), :cols] = line
        return 0

    lax.fori_loop(0, rows // many, norm, 0)
    mine = pl.ds(pl.multiple_of(place * rows, rows), rows)
    tiles[mine, :] = jnp.concatenate(
        [bias_f32[pl.ds(h, rows, stride=8), :][:, :cols] for h in range(heads)], axis=1
    ).astype(jnp.bfloat16)

    pl.semaphore_wait(barrier, members + 2)
    for step in range(1, members // 2):
        there = lax.rem(row + 2 * step, members)
        send(tiles.at[mine], tiles.at[mine], t_send, t_recv, (there, col))

    def turn(t, _):
        for u in range(many):
            j = t * many + u
            sent[j] = normed[pl.ds(j, rows, stride=cols), :].astype(jnp.bfloat16)
        return 0

    lax.fori_loop(0, cols // many, turn, 0)
    here = pl.ds(pl.multiple_of(slot * rows, rows), rows)
    for g in range(ncol // GROUP):
        def scatter(step, _, g=g):
            peer = lax.rem(row + step, members)
            send(
                sent.at[pl.ds(peer * ncol + g * GROUP, GROUP)],
                x_ref.at[pl.ds(g * GROUP, GROUP), here],
                in_send, in_recv.at[g], (peer, col),
            )
            return 0

        lax.fori_loop(1, members, scatter, 0)
    for j in range(ncol):
        x_ref[j, here, :] = sent[row * ncol + j]

    await_bytes(tiles.at[pl.ds(0, (members // 2 - 1) * rows)], t_recv)
    wide = cols // 2
    packed = heads * cols
    eye = (
        lax.broadcasted_iota(jnp.int32, (packed, packed), 0) == lax.broadcasted_iota(jnp.int32, (packed, packed), 1)
    ).astype(jnp.bfloat16)
    turned = lax.dot_general(eye, tiles[...], NT, preferred_element_type=jnp.float32).astype(jnp.bfloat16)
    for h in range(heads):
        for part in range(2):
            at = pl.ds(pl.multiple_of(x * cols + y_hi * wide, wide), wide)
            bias[h, core, part, at, :] = turned[h * cols + part * wide : h * cols + (part + 1) * wide]

    def owned(h, owner, side):
        return bias.at[h, core, :, pl.ds(pl.multiple_of(owner * cols + side * wide, wide), wide)]

    near, far = y_hi, 1 - y_hi

    def offer(h, side, n):
        block = owned(h, x, side)
        send(block, block, x1_send, x1_recv.at[h, 0, n], right)
        send(block, block, x1_send, x1_recv.at[h, 1, n], left)
        send(block, block, sib_send, sib_recv.at[h, n], sibling)

    def offer_far(h):
        await_bytes(owned(h, x, far), y_recv.at[h])
        offer(h, far, 1)

    for h in range(heads):
        block = owned(h, x, near)
        send(block, block, y_send, y_recv.at[h], across)
        if h < 2:
            offer(h, near, 0)
    offer_far(0)
    offer(2, near, 0)
    offer_far(1)
    offer(3, near, 0)
    offer_far(2)
    offer_far(3)

    def forward(h):
        for n, (owner, ahead) in enumerate(((x_left, right), (x_right, left))):
            for m, part in enumerate((near, far)):
                block = owned(h, owner, part)
                await_bytes(block, x1_recv.at[h, n, m])
                if n == m:
                    send(block, block, x2_send, x2_recv.at[h, n], ahead)
                send(block, block, sib_send, sib_recv.at[h, 2 + 2 * n + m], sibling)

    def pass_on(h):
        for n, side in enumerate((near, far)):
            block = owned(h, x_far, side)
            await_bytes(block, x2_recv.at[h, n])
            send(block, block, sib_send, sib_recv.at[h, 6 + n], sibling)

    def complete(h):
        for n in range(8):
            await_bytes(owned(h, x, near), sib_recv.at[h, n])

    lane = lax.broadcasted_iota(jnp.int32, (count, width), 1) // head_dim
    one = (lax.broadcasted_iota(jnp.int32, (count, width), 1) == 0).astype(jnp.bfloat16)

    def order(tokens):
        line = tokens.reshape(1, count)
        places = [2 * n + c for c in range(2) for n in range(members // 2)]
        return jnp.concatenate([line[:, n * rows : (n + 1) * rows] for n in places], axis=1)

    real, chains = order(token_ref[...]) == 1, order(chains_ref[...])
    wkt = wk_ref[...].astype(jnp.float32).T.astype(jnp.bfloat16)

    def project(j, _):
        block = x_ref[j]
        q = jnp.dot(block, wq_ref[...], preferred_element_type=jnp.float32)
        q_s[j] = (q * (LOG2E / math.sqrt(head_dim))).astype(jnp.bfloat16)
        g_s[j] = jax.nn.sigmoid(jnp.dot(block, wg_ref[...], preferred_element_type=jnp.float32))
        kt[j, :width, :] = lax.dot_general(wkt, block, NT, preferred_element_type=jnp.float32).astype(
            jnp.bfloat16
        )
        first = lax.broadcasted_iota(jnp.int32, (16, count), 0) == 0
        chain = chain_ref[col * cols + row * ncol + j]
        keep = real & (chains == chain)
        kt[j, width : width + 16, :] = jnp.where(first & ~keep, NEG, 0.0).astype(jnp.bfloat16)
        kt[j, width + 16 :, :] = jnp.zeros((width - 16, count), jnp.bfloat16)
        va[j, :, :width] = jnp.dot(block, wv_ref[...], preferred_element_type=jnp.float32).astype(jnp.bfloat16)
        va[j, :, width:] = jnp.ones((count, width), jnp.bfloat16)
        return 0

    for g in range(ncol // GROUP):
        await_bytes(x_ref.at[pl.ds(0, GROUP), pl.ds(0, count - rows)], in_recv.at[g])
        lax.fori_loop(g * GROUP, (g + 1) * GROUP, project, 0)
        if g == 0:
            forward(0)

    lanes = jnp.concatenate([lane, lane], 1)

    def scores(h, j):
        q = jnp.where(lane == h, q_s[j], jnp.zeros((count, width), jnp.bfloat16))
        s = jnp.dot(jnp.concatenate([q, one], 1), kt[j], preferred_element_type=jnp.float32)
        b = jnp.concatenate([bias[h, n].reshape(count, half) for n in range(2)], 1)
        return s + b.astype(jnp.float32) * LOG2E

    def settle(s, h, j):
        peak = jnp.max(s, axis=1, keepdims=True)
        p = jnp.exp2(s - peak).astype(jnp.bfloat16)
        o = jnp.dot(p, va[j], preferred_element_type=jnp.float32)
        acc[j] = jnp.where(lanes == h, o, acc[j])

    def early(t, _):
        for u in range(2):
            now = 2 * t + u
            later = now + 1
            ahead = scores(later // ncol, lax.rem(later, ncol))
            settle(score[u], now // ncol, lax.rem(now, ncol))
            score[1 - u] = ahead
        return 0

    def late(j, _):
        ahead = scores(heads - 1, j)
        settle(score[0], heads - 2, j)
        score[1] = ahead
        ahead = scores(heads - 2, jnp.minimum(j + 1, ncol - 1))
        settle(score[1], heads - 1, j)
        score[0] = ahead
        o = acc[j]
        gated = (o[:, :width] / o[:, width:] * g_s[j]).astype(jnp.bfloat16)
        back[j] = jnp.dot(gated, wo_ref[...], preferred_element_type=jnp.float32).astype(jnp.bfloat16)

        def give(step, _):
            peer = lax.rem(row + step, members)
            at = (lax.rem(peer, 2) * (members // 2) + peer // 2) * rows
            send(
                back.at[j, pl.ds(pl.multiple_of(at, rows), rows)], out_ref.at[row * ncol + j],
                out_send, out_recv, (peer, col),
            )
            return 0

        lax.fori_loop(1, members, give, 0)
        out_ref[row * ncol + j] = back[j, here, :]
        return 0

    pass_on(0)
    forward(1)
    complete(0)
    score[0] = scores(0, 0)
    lax.fori_loop(0, 2, early, 0)
    pass_on(1)
    forward(2)
    complete(1)
    lax.fori_loop(2, 5, early, 0)
    pass_on(2)
    forward(3)
    complete(2)
    lax.fori_loop(5, 6, early, 0)
    pass_on(3)
    complete(3)
    lax.fori_loop(0, ncol, late, 0)

    await_bytes(out_ref.at[pl.ds(0, (members - 1) * ncol)], out_recv)
    await_bytes(out_ref.at[pl.ds(0, (members - 1) * ncol)], out_send)
    await_bytes(sent.at[pl.ds(0, (members - 1) * ncol)], in_send)
    await_bytes(tiles.at[pl.ds(0, (members // 2 - 1) * rows)], t_send)
    await_bytes(bias.at[0, 0, 0], y_send)
    await_bytes(bias.at[0], x1_send)
    await_bytes(bias.at[0, 0], x2_send)
    await_bytes(bias.at[:, 0], sib_send)


def exchange(heads, ncol, count, pair, token_mask, chain_ids, *weights):
    rows, cols, width = pair.shape
    half = count // 2
    bf16, f32 = jnp.bfloat16, jnp.float32
    dma = pltpu.SemaphoreType.DMA
    return pl.pallas_call(
        functools.partial(kernel, heads),
        out_shape=jax.ShapeDtypeStruct((cols, rows, width), bf16),
        in_specs=[pl.BlockSpec(memory_space=pltpu.SMEM if n == 3 else pltpu.VMEM) for n in range(10)],
        out_specs=pl.BlockSpec(memory_space=pltpu.VMEM),
        scratch_shapes=[
            pltpu.VMEM((rows * cols, width), f32),
            pltpu.VMEM((rows * 8, 128), f32),
            pltpu.VMEM((cols, rows, width), bf16),
            pltpu.VMEM((ncol, count, width), bf16),
            pltpu.VMEM((half, heads * cols), bf16),
            pltpu.VMEM((heads, 2, 2, half, half), bf16),
            pltpu.VMEM((ncol, count, width), bf16),
            pltpu.VMEM((ncol, count, width), f32),
            pltpu.VMEM((ncol, 2 * width, count), bf16),
            pltpu.VMEM((ncol, count, 2 * width), bf16),
            pltpu.VMEM((ncol, count, 2 * width), f32),
            pltpu.VMEM((2, count, count), f32),
            pltpu.VMEM((ncol, count, width), bf16),
            dma, dma((ncol // GROUP,)), dma, dma, dma, dma((heads,)), dma, dma((heads, 2, 2)), dma, dma((heads, 2)),
            dma, dma((heads, 8)), dma, dma,
        ],
        compiler_params=pltpu.CompilerParams(
            collective_id=0, has_side_effects=True, vmem_limit_bytes=56 * 2**20
        ),
        cost_estimate=pl.CostEstimate(flops=4 * 10**9, bytes_accessed=10**7, transcendentals=15 * 10**6),
    )(pair, token_mask, chain_ids, chain_ids, *weights)


def body(pair, token_mask, chain_ids, w_query, w_key, w_value, w_gate, w_bias, w_out):
    rows, cols, width = pair.shape
    heads = w_bias.shape[1]
    count = token_mask.shape[0]
    members = count // rows
    ncol = cols // members
    update = exchange(
        heads, ncol, count, pair, token_mask, chain_ids, w_query, w_key, w_value, w_gate, w_bias.T, w_out
    )
    return jnp.swapaxes(update, 0, 1)


def solution(mesh):
    placed = (P("row", "col", None), P(), P(), P(), P(), P(), P(), P(), P())
    return jax.shard_map(
        body, mesh=mesh, in_specs=placed, out_specs=P("row", "col", None), check_vma=False
    )
```

time: 99.1 us -> 72 us (0.73)
  Pallas kernels: 88.8 us -> 69.2 us
  local copies, waits for them, and re-layouts: 7.12 us -> 2.59 us
  other arithmetic: 2.78 us -> 0 us
    pallas_call x1, Pallas kernels: 88.8 us -> 69.2 us  [exchange(): pl.pallas_call(functools.partial(kernel, heads), out_shape=jax.ShapeDtype...]
    unnamed x1 -> x0, local copies, waits for them, and re-layouts: 1.46 us -> none
    concatenate x1 -> x0, other arithmetic: 1.41 us -> none  [body(): wqg = jnp.concatenate([w_query, w_gate], 1)]
    pad x1 -> x0, local copies, waits for them, and re-layouts: 1.29 us -> none  [body(): wbt = jnp.pad(w_bias.T, ((0, 16 - heads), (0, 0)))]
where the time goes in v3:
time: 72 us; the launch traced here: 71.8 us
  Pallas kernels  69.2 us (96%)
  local copies, waits for them, and re-layouts  2.59 us (4%)
    pallas_call x1, Pallas kernels, exchange(): pl.pallas_call(functools.partial(kernel, heads), out_shape=jax.ShapeDtype...  69.2 us
    transpose x1, local copies, waits for them, and re-layouts, body(): return jnp.swapaxes(update, 0, 1)  2.59 us

profile of v3, /device:TPU:1, one launch (start us, length us, event | category | flops | bytes accessed | tf_op | source)
XLA Modules:
  0.0 71.8 jit_solution(9539132643434410963)
XLA Ops:
  0.0 69.2 %shard_map.91 = bf16[96,48,128]{2,1,0:T(8,128)(2,1)} custom-call(bf16[48,96,128]{2,1,0:T(8,128)(2,1)} %pair_ref.1, s32[768]{0:T(1024)} %token_ref.1, s32[768]{0:T(1024)} %chain_ref.1, s32[768]{0:T(1024)} %chain_ref.1, bf16[128,128]{1,0:T(8,128)(2,1)} %wq_ref.1, bf16[128,128]{1,0:T(8,128)(2,1)} %wk_ref.1, bf16[128,128]{1,0:T(8,128)(2,1)} %wv_ref.1, ...), custom_call_target="tpu_custom_call" | custom-call | flops 4000000000 | bytes 10000000 | tf_op jit(solution)/shard_map/pallas_call | solution.py:281
  69.2 2.6 %copy.10 = bf16[48,96,128]{2,1,0:T(8,128)(2,1)} copy(bf16[48,96,128]{2,0,1:T(8,128)(2,1)} %bitcast.2) | data formatting | bytes 2359296 | tf_op jit(solution)/shard_map/transpose | solution.py:319

commit v4 on v3

--- a/solution.py
+++ b/solution.py
@@ -21,7 +21,7 @@
     pair_ref, token_ref, chains_ref, chain_ref, wq_ref, wk_ref, wv_ref, wg_ref, wb_ref, wo_ref, out_ref,
     normed, bias_f32, sent, x_ref, tiles, bias, q_s, g_s, kt, va, acc, score, back,
     in_send, in_recv, t_send, t_recv, y_send, y_recv, x1_send, x1_recv, x2_send, x2_recv,
-    sib_send, sib_recv, out_send, out_recv,
+    up_send, down_send, z_recv, sib_send, sib_recv, out_send, out_recv,
 ):
     rows, cols, width = pair_ref.shape
     ncol, count, _ = x_ref.shape
@@ -41,6 +41,11 @@
     there = lax.rem(y + 3 - 2 * y_lo, 4)
     across = ((lax.rem(there, 2) * Z + z) * 2 + core, x * 2 + there // 2)
 
+    up, down = (row - 2 * z + 2 * lax.rem(z + 1, Z), col), (row - 2 * z + 2 * lax.rem(z + Z - 1, Z), col)
+
+    def head_at(n):
+        return 2 * lax.rem(z + lax.rem(n, 2), 2) + n // 2
+
     def send(src, dst, send_sem, recv_sem, device):
         pltpu.make_async_remote_copy(
             src_ref=src, dst_ref=dst, send_sem=send_sem, recv_sem=recv_sem, device_id=device, device_id_type=MESH
@@ -60,7 +65,7 @@
         pl.semaphore_signal(barrier, inc=1, device_id=device, device_id_type=MESH)
 
     bias_f32[...] = jnp.zeros_like(bias_f32)
-    many = 4
+    many = rows // 4
 
     def norm(t, _):
         values = pair_ref[pl.ds(t * many, many)].reshape(many * cols, width).astype(jnp.float32)
@@ -86,12 +91,12 @@
         send(tiles.at[mine], tiles.at[mine], t_send, t_recv, (there, col))
 
     def turn(t, _):
-        for u in range(many):
-            j = t * many + u
+        for u in range(cols // 8):
+            j = t * (cols // 8) + u
             sent[j] = normed[pl.ds(j, rows, stride=cols), :].astype(jnp.bfloat16)
         return 0
 
-    lax.fori_loop(0, cols // many, turn, 0)
+    lax.fori_loop(0, 8, turn, 0)
     here = pl.ds(pl.multiple_of(slot * rows, rows), rows)
     for g in range(ncol // GROUP):
         def scatter(step, _, g=g):
@@ -124,46 +129,62 @@
 
     near, far = y_hi, 1 - y_hi
 
-    def offer(h, side, n):
+    def offer(n, side, m):
+        h = head_at(n)
         block = owned(h, x, side)
-        send(block, block, x1_send, x1_recv.at[h, 0, n], right)
-        send(block, block, x1_send, x1_recv.at[h, 1, n], left)
-        send(block, block, sib_send, sib_recv.at[h, n], sibling)
-
-    def offer_far(h):
+        if n % 2 == 0:
+            send(block, block, x1_send, x1_recv.at[h, 0, m], right)
+            send(block, block, x1_send, x1_recv.at[h, 1, m], left)
+        send(block, block, sib_send, sib_recv.at[h, m], sibling)
+
+    def offer_far(n):
+        h = head_at(n)
         await_bytes(owned(h, x, far), y_recv.at[h])
-        offer(h, far, 1)
-
-    for h in range(heads):
-        block = owned(h, x, near)
-        send(block, block, y_send, y_recv.at[h], across)
-        if h < 2:
-            offer(h, near, 0)
-    offer_far(0)
-    offer(2, near, 0)
-    offer_far(1)
-    offer(3, near, 0)
-    offer_far(2)
-    offer_far(3)
-
-    def forward(h):
+        offer(n, far, 1)
+
+    for n in (0, 2, 1, 3):
+        block = owned(head_at(n), x, near)
+        send(block, block, y_send, y_recv.at[head_at(n)], across)
+        offer(n, near, 0)
+    for n in (0, 2, 1, 3):
+        offer_far(n)
+
+    def relay(h, block, n, m):
+        send(block, block, sib_send, sib_recv.at[h, 2 + 2 * n + m], sibling)
+        if m == 0:
+            send(block, block, up_send, z_recv.at[h, n, m], up)
+        else:
+            send(block, block, down_send, z_recv.at[h, n, m], down)
+
+    def forward(n):
+        h = head_at(n)
         for n, (owner, ahead) in enumerate(((x_left, right), (x_right, left))):
             for m, part in enumerate((near, far)):
                 block = owned(h, owner, part)
                 await_bytes(block, x1_recv.at[h, n, m])
                 if n == m:
                     send(block, block, x2_send, x2_recv.at[h, n], ahead)
+                relay(h, block, n, m)
+
+    def pass_on(n):
+        h = head_at(n)
+        for m, part in enumerate((near, far)):
+            block = owned(h, x_far, part)
+            await_bytes(block, x2_recv.at[h, m])
+            relay(h, block, 2, m)
+
+    def accept(n):
+        h = head_at(n)
+        for n, owner in enumerate((x_left, x_right, x_far)):
+            for m, part in enumerate((near, far)):
+                block = owned(h, owner, part)
+                await_bytes(block, z_recv.at[h, n, m])
                 send(block, block, sib_send, sib_recv.at[h, 2 + 2 * n + m], sibling)
 
-    def pass_on(h):
-        for n, side in enumerate((near, far)):
-            block = owned(h, x_far, side)
-            await_bytes(block, x2_recv.at[h, n])
-            send(block, block, sib_send, sib_recv.at[h, 6 + n], sibling)
-
-    def complete(h):
-        for n in range(8):
-            await_bytes(owned(h, x, near), sib_recv.at[h, n])
+    def complete(n):
+        h = head_at(n)
+        for m in range(8):
+            await_bytes(owned(h, x, near), sib_recv.at[h, m])
 
     lane = lax.broadcasted_iota(jnp.int32, (count, width), 1) // head_dim
     one = (lax.broadcasted_iota(jnp.int32, (count, width), 1) == 0).astype(jnp.bfloat16)
@@ -198,6 +219,9 @@
         lax.fori_loop(g * GROUP, (g + 1) * GROUP, project, 0)
         if g == 0:
             forward(0)
+        if g == 1:
+            pass_on(0)
+            forward(2)
 
     lanes = jnp.concatenate([lane, lane], 1)
 
@@ -217,17 +241,17 @@
         for u in range(2):
             now = 2 * t + u
             later = now + 1
-            ahead = scores(later // ncol, lax.rem(later, ncol))
-            settle(score[u], now // ncol, lax.rem(now, ncol))
+            ahead = scores(head_at(later // ncol), lax.rem(later, ncol))
+            settle(score[u], head_at(now // ncol), lax.rem(now, ncol))
             score[1 - u] = ahead
         return 0
 
     def late(j, _):
-        ahead = scores(heads - 1, j)
-        settle(score[0], heads - 2, j)
+        ahead = scores(head_at(heads - 1), j)
+        settle(score[0], head_at(heads - 2), j)
         score[1] = ahead
-        ahead = scores(heads - 2, jnp.minimum(j + 1, ncol - 1))
-        settle(score[1], heads - 1, j)
+        ahead = scores(head_at(heads - 2), jnp.minimum(j + 1, ncol - 1))
+        settle(score[1], head_at(heads - 1), j)
         score[0] = ahead
         o = acc[j]
         gated = (o[:, :width] / o[:, width:] * g_s[j]).astype(jnp.bfloat16)
@@ -246,20 +270,18 @@
         out_ref[row * ncol + j] = back[j, here, :]
         return 0
 
-    pass_on(0)
-    forward(1)
     complete(0)
-    score[0] = scores(0, 0)
-    lax.fori_loop(0, 2, early, 0)
-    pass_on(1)
-    forward(2)
+    score[0] = scores(head_at(0), 0)
+    lax.fori_loop(0, 1, early, 0)
+    accept(1)
+    pass_on(2)
+    lax.fori_loop(1, 2, early, 0)
     complete(1)
-    lax.fori_loop(2, 5, early, 0)
-    pass_on(2)
-    forward(3)
+    lax.fori_loop(2, 4, early, 0)
+    accept(3)
+    lax.fori_loop(4, 5, early, 0)
     complete(2)
     lax.fori_loop(5, 6, early, 0)
-    pass_on(3)
     complete(3)
     lax.fori_loop(0, ncol, late, 0)
 
@@ -268,8 +290,10 @@
     await_bytes(sent.at[pl.ds(0, (members - 1) * ncol)], in_send)
     await_bytes(tiles.at[pl.ds(0, (members // 2 - 1) * rows)], t_send)
     await_bytes(bias.at[0, 0, 0], y_send)
-    await_bytes(bias.at[0], x1_send)
-    await_bytes(bias.at[0, 0], x2_send)
+    await_bytes(bias.at[0, 0], x1_send)
+    await_bytes(bias.at[0, 0, 0], x2_send)
+    await_bytes(bias.at[0, 0, :, pl.ds(0, 3 * cols)], up_send)
+    await_bytes(bias.at[0, 0, :, pl.ds(0, 3 * cols)], down_send)
     await_bytes(bias.at[:, 0], sib_send)
 
 
@@ -298,7 +322,7 @@
             pltpu.VMEM((2, count, count), f32),
             pltpu.VMEM((ncol, count, width), bf16),
             dma, dma((ncol // GROUP,)), dma, dma, dma, dma((heads,)), dma, dma((heads, 2, 2)), dma, dma((heads, 2)),
-            dma, dma((heads, 8)), dma, dma,
+            dma, dma, dma((heads, 3, 2)), dma, dma((heads, 8)), dma, dma,
         ],
         compiler_params=pltpu.CompilerParams(
             collective_id=0, has_side_effects=True, vmem_limit_bytes=56 * 2**20

time: 72 us -> 63 us (0.88)
  Pallas kernels: 69.2 us -> 60.2 us
    pallas_call x1, Pallas kernels: 69.2 us -> 60.2 us  [exchange(): pl.pallas_call(functools.partial(kernel, heads), out_shape=jax.ShapeDtype...]
where the time goes in v4:
time: 63 us; the launch traced here: 62.8 us
  Pallas kernels  60.2 us (96%)
  local copies, waits for them, and re-layouts  2.59 us (4%)
    pallas_call x1, Pallas kernels, exchange(): pl.pallas_call(functools.partial(kernel, heads), out_shape=jax.ShapeDtype...  60.2 us
    transpose x1, local copies, waits for them, and re-layouts, body(): return jnp.swapaxes(update, 0, 1)  2.59 us

profile of v4, /device:TPU:1, one launch (start us, length us, event | category | flops | bytes accessed | tf_op | source)
XLA Modules:
  0.0 62.8 jit_solution(6174410447031570781)
XLA Ops:
  0.0 60.2 %shard_map.91 = bf16[96,48,128]{2,1,0:T(8,128)(2,1)} custom-call(bf16[48,96,128]{2,1,0:T(8,128)(2,1)} %pair_ref.1, s32[768]{0:T(1024)} %token_ref.1, s32[768]{0:T(1024)} %chain_ref.1, s32[768]{0:T(1024)} %chain_ref.1, bf16[128,128]{1,0:T(8,128)(2,1)} %wq_ref.1, bf16[128,128]{1,0:T(8,128)(2,1)} %wk_ref.1, bf16[128,128]{1,0:T(8,128)(2,1)} %wv_ref.1, ...), custom_call_target="tpu_custom_call" | custom-call | flops 4000000000 | bytes 10000000 | tf_op jit(solution)/shard_map/pallas_call | solution.py:305
  60.2 2.6 %copy.10 = bf16[48,96,128]{2,1,0:T(8,128)(2,1)} copy(bf16[48,96,128]{2,0,1:T(8,128)(2,1)} %bitcast.2) | data formatting | bytes 2359296 | tf_op jit(solution)/shard_map/transpose | solution.py:343

commit v5 on v4

--- a/solution.py
+++ b/solution.py
@@ -65,7 +65,7 @@
         pl.semaphore_signal(barrier, inc=1, device_id=device, device_id_type=MESH)
 
     bias_f32[...] = jnp.zeros_like(bias_f32)
-    many = rows // 4
+    many = rows // 3
 
     def norm(t, _):
         values = pair_ref[pl.ds(t * many, many)].reshape(many * cols, width).astype(jnp.float32)

time: 63 us -> 62.5 us (level)
  no operation moved by 1% of the time
where the time goes in v5:
time: 62.5 us; the launch traced here: 62.3 us
  Pallas kernels  59.7 us (96%)
  local copies, waits for them, and re-layouts  2.59 us (4%)
    pallas_call x1, Pallas kernels, exchange(): pl.pallas_call(functools.partial(kernel, heads), out_shape=jax.ShapeDtype...  59.7 us
    transpose x1, local copies, waits for them, and re-layouts, body(): return jnp.swapaxes(update, 0, 1)  2.59 us

profile of v5, /device:TPU:1, one launch (start us, length us, event | category | flops | bytes accessed | tf_op | source)
XLA Modules:
  0.0 62.3 jit_solution(7663571920663050895)
XLA Ops:
  0.0 59.7 %shard_map.91 = bf16[96,48,128]{2,1,0:T(8,128)(2,1)} custom-call(bf16[48,96,128]{2,1,0:T(8,128)(2,1)} %pair_ref.1, s32[768]{0:T(1024)} %token_ref.1, s32[768]{0:T(1024)} %chain_ref.1, s32[768]{0:T(1024)} %chain_ref.1, bf16[128,128]{1,0:T(8,128)(2,1)} %wq_ref.1, bf16[128,128]{1,0:T(8,128)(2,1)} %wk_ref.1, bf16[128,128]{1,0:T(8,128)(2,1)} %wv_ref.1, ...), custom_call_target="tpu_custom_call" | custom-call | flops 4000000000 | bytes 10000000 | tf_op jit(solution)/shard_map/pallas_call | solution.py:305
  59.7 2.6 %copy.10 = bf16[48,96,128]{2,1,0:T(8,128)(2,1)} copy(bf16[48,96,128]{2,0,1:T(8,128)(2,1)} %bitcast.2) | data formatting | bytes 2359296 | tf_op jit(solution)/shard_map/transpose | solution.py:343
